TPU v7x, 32 devices: a whole 2x2x4 slice. The times are simulated.
32 devices in a mesh: req: 4 (over y, x), mlp: 8 (over z, core).
Axes of the slice: x: 2, y: 2, z: 4, core: 2. Of those that a mesh axis runs over, the one named last changes fastest.
Arguments:
- hidden: bfloat16 [8, 5, 4096], P('req', None, 'mlp'), may hold values from -6 to 6
- attn_gain: float32 [4096], P('mlp'), may hold values from 0.1 to 1.9
- w_qkv: bfloat16 [4096, 6144], P('mlp'), may hold values from -0.09375 to 0.09375
- w_out: bfloat16 [4096, 4096], P(None, 'mlp'), may hold values from -0.09375 to 0.09375
- mlp_gain: float32 [4096], replicated, may hold values from 0.1 to 1.9
- w_gate: bfloat16 [4096, 14336], P(None, ('req', 'mlp')), may hold values from -0.09375 to 0.09375
- w_up: bfloat16 [4096, 14336], P(None, ('req', 'mlp')), may hold values from -0.09375 to 0.09375
- w_down: bfloat16 [14336, 4096], P(('req', 'mlp')), may hold values from -0.09375 to 0.09375
- kv_cache: bfloat16 [8, 1024, 2048], P('req', 'mlp')
- lengths: int32 [8], P('req'), may hold values from 1 to 1024, as said below
- mig_slot: int32 [4], replicated, may hold values from 0 to 1, as said below
- mig_dest: int32 [4], replicated, may hold values from 0 to 3, each once
Outputs:
- layer_out: bfloat16 [8, 5, 4096], P('req', None, 'mlp')
- moved_cache: bfloat16 [4, 128, 2048], P('req', 'mlp')
Inputs may be any that keep to these rules, and one draw needn't show every extreme that they name: `mig_slot`: the slot of each group that its leaving request vacates and the arriving one takes. `mig_dest`: A permutation of the groups: every group receives exactly one request. `lengths`: in slot g * 2 + mig_slot[g] the length is at most 128, reached in some group; some slot has exactly 1024.
All inputs are finite; a program needn't handle non-finite values.
Results may differ from a plain program's by a relative error of at most 0.012.
The roundings to bfloat16 on the way count: a program that leaves them out, or rounds other values in their place, can miss the bound.
Values may be sent and summed in bfloat16 or wider, within the bound.
A program may use at most 128 MiB of HBM per device.

v0:
```python
import jax
import jax.numpy as jnp
from jax import lax
from jax.sharding import PartitionSpec as P

D = 4096
HEADS = 32
KVH = 8
HD = 128
MIG_ROWS = 16


EPSILON = 1e-05
ROPE_BASE = 500000.0
NEG_FILL = -1e30


def merged_2(shard, axis, combine):
    everything = jax.tree.map(lambda part: lax.all_gather(part, axis), shard)
    initial = jax.tree.map(lambda part: part[0], everything)

    def lap(k, so_far):
        return combine(so_far, jax.tree.map(lambda part: part[k], everything))

    return lax.fori_loop(1, lax.axis_size(axis), lap, initial)


def rotate(vectors, positions):
    half_dim = vectors.shape[-1] // 2
    frequency = ROPE_BASE ** (-(jnp.arange(half_dim).astype(jnp.float32) / half_dim))
    angles = positions.astype(jnp.float32)[..., None, None] * frequency
    cos_part = jnp.cos(angles)
    sin_part = jnp.sin(angles)
    leading = vectors[..., :half_dim]
    trailing = vectors[..., half_dim:]
    return jnp.concatenate(
        [leading * cos_part - trailing * sin_part, trailing * cos_part + leading * sin_part],
        axis=-1,
    )


def combine(former, latter):
    former_max, former_sum, former_acc = former
    latter_max, latter_sum, latter_acc = latter
    highest = jnp.maximum(former_max, latter_max)
    former_rate = jnp.exp(former_max - highest)
    latter_rate = jnp.exp(latter_max - highest)
    return (
        highest,
        former_sum * former_rate + latter_sum * latter_rate,
        former_acc * former_rate[..., None] + latter_acc * latter_rate[..., None],
    )


def softmax_part(scores, usable, values, pattern):
    highest = jnp.max(jnp.where(usable, scores, NEG_FILL), axis=-1)
    weights = jnp.where(usable, jnp.exp(scores - highest[..., None]), 0.0)
    mixture = jnp.einsum(
        pattern, weights.astype(jnp.bfloat16), values, preferred_element_type=jnp.float32
    )
    return (highest, jnp.sum(weights, axis=-1), mixture)


def body(
    hidden,
    attn_gain,
    w_qkv,
    w_out,
    mlp_gain,
    w_gate,
    w_up,
    w_down,
    kv_cache,
    lengths,
    mig_slot,
    mig_dest,
):
    group_count = lax.axis_size("req")
    block_count = lax.axis_size("mlp")
    group_id = lax.axis_index("req")
    block_id = lax.axis_index("mlp")
    slot_count, spec_len, width_dev = hidden.shape
    ctx_dev = kv_cache.shape[1]
    kv_width = kv_cache.shape[2] // 2
    zero_index = jnp.zeros((), jnp.int32)
    own_slot = mig_slot[group_id]
    target = mig_dest[group_id]
    source = jnp.sum(jnp.where(mig_dest == group_id, jnp.arange(group_count, dtype=jnp.int32), 0))
    leaving = lax.dynamic_index_in_dim(kv_cache, own_slot, 0, keepdims=False)[:MIG_ROWS]
    outgoing = jnp.zeros((group_count,) + leaving.shape, leaving.dtype)
    outgoing = lax.dynamic_update_slice(outgoing, leaving[None], (target, zero_index, zero_index))
    incoming = lax.all_to_all(outgoing, "req", split_axis=0, concat_axis=0, tiled=True)
    arrived = lax.dynamic_index_in_dim(incoming, source, 0, keepdims=False)
    live_cache = lax.dynamic_update_slice(
        kv_cache, arrived[None], (own_slot, zero_index, zero_index)
    )
    widened = hidden.astype(jnp.float32)
    square_part = jnp.sum(widened * widened, axis=-1)
    scaled = (widened * attn_gain).astype(jnp.bfloat16)
    projected = jnp.einsum("rsd,de->rse", scaled, w_qkv, preferred_element_type=jnp.float32)
    square_sum, projected = lax.psum((square_part, projected), "mlp")
    projected = projected * lax.rsqrt(square_sum / D + EPSILON)[..., None]
    positions = lengths[:, None] + jnp.arange(spec_len, dtype=jnp.int32)[None, :]
    query_width = HEADS * HD
    queries = rotate(
        projected[..., :query_width].reshape(slot_count, spec_len, HEADS, HD), positions
    ).astype(jnp.bfloat16)
    new_keys = rotate(
        projected[..., query_width : query_width + kv_width].reshape(slot_count, spec_len, KVH, HD),
        positions,
    ).astype(jnp.bfloat16)
    new_values = (
        projected[..., query_width + kv_width :]
        .reshape(slot_count, spec_len, KVH, HD)
        .astype(jnp.bfloat16)
    )
    grouped = queries.reshape(slot_count, spec_len, KVH, HEADS // KVH, HD)
    score_scale = HD ** (-0.5)
    cached_keys = live_cache[..., :kv_width].reshape(slot_count, ctx_dev, KVH, HD)
    cached_values = live_cache[..., kv_width:].reshape(slot_count, ctx_dev, KVH, HD)
    scores = (
        jnp.einsum("rsgqd,rcgd->rgsqc", grouped, cached_keys, preferred_element_type=jnp.float32)
        * score_scale
    )
    stored = jnp.arange(ctx_dev, dtype=jnp.int32) * block_count + block_id
    usable = (stored[None, :] < lengths[:, None])[:, None, None, None, :]
    block_part = softmax_part(scores, usable, cached_values, "rgsqc,rcgd->rgsqd")
    merged = merged_2(block_part, "mlp", combine)
    own_scores = (
        jnp.einsum("rsgqd,rtgd->rgsqt", grouped, new_keys, preferred_element_type=jnp.float32)
        * score_scale
    )
    causal = (jnp.arange(spec_len)[:, None] >= jnp.arange(spec_len)[None, :])[
        None, None, :, None, :
    ]
    own_part = softmax_part(own_scores, causal, new_values, "rgsqt,rtgd->rgsqd")
    highest, summed, mixture = combine(merged, own_part)
    attended = (
        (mixture / summed[..., None])
        .transpose(0, 2, 1, 3, 4)
        .reshape(slot_count, spec_len, query_width)
        .astype(jnp.bfloat16)
    )
    residual = (
        widened + jnp.einsum("rse,ed->rsd", attended, w_out, preferred_element_type=jnp.float32)
    ).astype(jnp.bfloat16)
    gathered = lax.all_gather(residual[None], ("req", "mlp"), axis=0, tiled=True)
    token_group = slot_count * spec_len
    gathered = gathered.reshape(group_count, block_count, token_group, width_dev)
    widened_rows = gathered.astype(jnp.float32)
    inverse = lax.rsqrt(jnp.sum(widened_rows * widened_rows, axis=(1, 3)) / D + EPSILON)
    scaled_rows = (widened_rows * mlp_gain.reshape(block_count, 1, width_dev)).astype(jnp.bfloat16)
    hidden_dev = w_gate.shape[1]
    gate_proj = (
        jnp.einsum(
            "rmtc,mcf->rtf",
            scaled_rows,
            w_gate.reshape(block_count, width_dev, hidden_dev),
            preferred_element_type=jnp.float32,
        )
        * inverse[..., None]
    )
    up_proj = (
        jnp.einsum(
            "rmtc,mcf->rtf",
            scaled_rows,
            w_up.reshape(block_count, width_dev, hidden_dev),
            preferred_element_type=jnp.float32,
        )
        * inverse[..., None]
    )
    activated = (jax.nn.silu(gate_proj) * up_proj).astype(jnp.bfloat16)
    down_cols = w_down.reshape(hidden_dev, block_count, width_dev)
    block_index = jnp.arange(
        lax.axis_size(("req", "mlp")) * token_group // token_group, dtype=jnp.int32
    )
    row_sel = jnp.take(activated, block_index // block_count, axis=0)
    col_sel = jnp.take(down_cols, block_index % block_count, axis=1)
    product = jnp.einsum("ktf,fkc->ktc", row_sel, col_sel, preferred_element_type=jnp.float32)
    added = lax.psum_scatter(
        product.reshape(lax.axis_size(("req", "mlp")) * token_group, width_dev),
        ("req", "mlp"),
        scatter_dimension=0,
        tiled=True,
    )
    layer_out = (
        residual.astype(jnp.float32) + added.reshape(slot_count, spec_len, width_dev)
    ).astype(jnp.bfloat16)
    return (layer_out, arrived[None])


def solution(mesh):
    placed = (
        P("req", None, "mlp"),
        P("mlp"),
        P("mlp", None),
        P(None, "mlp"),
        P(),
        P(None, ("req", "mlp")),
        P(None, ("req", "mlp")),
        P(("req", "mlp"), None),
        P("req", "mlp", None),
        P("req"),
        P(),
        P(),
    )
    return jax.shard_map(
        body,
        mesh=mesh,
        in_specs=placed,
        out_specs=(P("req", None, "mlp"), P("req", "mlp", None)),
        check_vma=False,
    )
```

profile of v0, /device:TPU:0, one launch (start us, length us, event | category | flops | bytes accessed | tf_op | source)
XLA Modules:
  0.0 325.4 jit_solution(10649896896473231463)
XLA Ops:
  7.3 4.6 %fusion.9 = f32[2,5,6144]{2,1,0:T(8,128)} fusion(bf16[512,6144]{1,0:T(8,128)(2,1)} %param.16, bf16[2,5,512]{2,0,1:T(2,128)(2,1)} %param.14, f32[512]{0:T(512)} %param.15), kind=kOutput, calls=%fused_computation.17 | convolution fusion | flops 62929920 | bytes 6549504 | tf_op jit(solution)/shard_map/rsd,de->rse/dot_general | solution.py:100
  17.0 0.7 broadcast_in_dim.99
  18.4 5.2 %all-to-all-start = ((bf16[4,16,2048]{2,1,0:T(8,128)(2,1)}), bf16[4,16,2048]{2,1,0:T(8,128)(2,1)S(1)}, u32[]{:S(2)}, u32[]{:S(2)}) async-start(bf16[4,16,2048]{2,1,0:T(8,128)(2,1)} %dynamic-slice_dynamic-update-slice_fusion), calls=%async_computation | async-start | bytes 524288 | tf_op jit(solution)/shard_map/all_to_all | solution.py:92
  23.6 0.7 copy.134
  24.3 0.6 fusion.56
  26.2 16.4 %psum.15 = f32[2,5]{1,0:T(2,128)S(1)} all-reduce(f32[2,5]{1,0:T(2,128)S(1)} %fusion.47), channel_id=1, replica_groups=mesh['req'=4,'mlp'=8] {'mlp'}, use_global_device_ids=true, to_apply=%region_2.3 | all-reduce | flops 10 | bytes 80 | tf_op jit(solution)/shard_map/psum | solution.py:101
  43.6 26.7 %all-reduce.4.cloned.1.call-done = f32[2,5,6144]{2,1,0:T(8,128)} async-done(((f32[2,5,6144]{2,1,0:T(8,128)}), f32[2,5,6144]{2,1,0:T(8,128)}) %all-reduce.4.cloned.1.call-update) | async-done | bytes 245776 | tf_op jit(solution)/shard_map/psum | solution.py:101
  70.3 1.1 broadcast_multiply_fusion
  72.1 2.0 dynamic_update_slice.7
  75.0 0.8 copy.139
  75.9 4.2 %copy.227 = bf16[56,8,8,512]{3,2,0,1:T(8,128)(2,1)} copy(bf16[56,8,8,512]{3,2,1,0:T(8,128)(2,1)} %bitcast.134) | data formatting | bytes 7340032 | tf_op jit(solution)/shard_map/reshape | solution.py:173
  80.1 9.3 %gather_fusion.1 = bf16[32,448,512]{2,1,0:T(8,128)(2,1)} fusion(bf16[448,8,512]{2,0,1:T(8,128)(2,1)} %bitcast.133, s32[1024]{0:T(1024)S(1)} %pad_clamp_fusion), kind=kCustom, calls=%fused_computation.1 | custom fusion | bytes 29360256 | tf_op jit(solution)/shard_map/jit(_take)/gather | solution.py:178
  89.6 0.7 fusion.48
  91.7 14.0 %all-gather = f32[16,8,5,4]{1,3,2,0:T(4,128)S(1)} all-gather(f32[2,8,5,4]{1,3,2,0:T(4,128)S(1)} %copy.136), channel_id=2, replica_groups=mesh['req'=4,'mlp'=8] {'mlp'}, dimensions={0}, use_global_device_ids=true | all-gather | bytes 11520 | tf_op jit(solution)/shard_map/all_gather | solution.py:19
  106.2 14.0 %all-gather.1 = f32[16,8,5,4]{1,3,2,0:T(4,128)S(1)} all-gather(f32[2,8,5,4]{1,3,2,0:T(4,128)S(1)} %copy.137), channel_id=3, replica_groups=mesh['req'=4,'mlp'=8] {'mlp'}, dimensions={0}, use_global_device_ids=true | all-gather | bytes 11520 | tf_op jit(solution)/shard_map/all_gather | solution.py:19
  120.2 0.9 slice.68
  121.2 12.6 %while.19 = (s32[]{:T(128)}, f32[2,8,5,4]{1,3,2,0:T(4,128)S(1)}, f32[2,8,5,4]{1,3,2,0:T(4,128)S(1)}, f32[2,8,5,4,128]{4,3,2,1,0:T(4,128)S(1)}, f32[8,2,8,5,4]{2,...) while((s32[]{:T(128)}, f32[2,8,5,4]{1,3,2,0:T(4,128)S(1)}, ...), condition=%wide.region_7.8_spmd, body=%wide.region_6.7_spmd.sunk | while | flops 124805 | bytes 837271 | solution.py:25
  121.2 0.9 constant_dynamic-slice_fusion.4
  123.0 0.9 constant_dynamic-slice_fusion.4
  124.8 0.9 constant_dynamic-slice_fusion.4
  126.6 0.9 constant_dynamic-slice_fusion.4
  128.4 0.9 constant_dynamic-slice_fusion.4
  130.2 0.9 constant_dynamic-slice_fusion.4
  132.0 0.9 constant_dynamic-slice_fusion.4
  134.4 2.9 fusion.29
  137.3 41.9 %all-gather.3 = bf16[64,5,512]{2,1,0:T(8,128)(2,1)S(1)} all-gather(bf16[2,5,512]{2,1,0:T(8,128)(2,1)S(1)} %fusion.29), channel_id=5, replica_groups=mesh['req'=4,'mlp'=8] {'req','mlp'}, dimensions={0}, use_global_device_ids=true | all-gather | bytes 337920 | tf_op jit(solution)/shard_map/all_gather | solution.py:147
  179.6 3.4 %fusion.24 = f32[4,10,448]{2,1,0:T(8,128)S(1)} fusion(bf16[56,8,8,512]{3,2,1,0:T(8,128)(2,1)} %bitcast.153, f32[4,8,10,512]{3,2,1,0:T(8,128)S(1)} %reshape.225, f32[8,512]{1,0:T(8,128)S(1)} %mul.286, f32[4,10]{1,0:T(4,128)S(1)} %add_rsqrt_fusion), kind=kOutput, calls=%fused_computation.37 | convolution fusion | flops 147146240 | bytes 4413600 | tf_op jit(solution)/shard_map/rmtc,mcf->rtf/dot_general | solution.py:155
  183.0 1.2 fusion.25
  184.8 6.5 %fusion.4 = f32[32,10,512]{2,1,0:T(8,128)S(1)} fusion(bf16[32,448,512]{2,1,0:T(8,128)(2,1)} %gather_fusion.1, pred[32]{0:T(512)(128)(4,1)S(1)} %get-tuple-element.263, bf16[32,10,448]{2,1,0:T(8,128)(2,1)S(1)} %gather_fusion, pred[32]{0:T(512)(128)(4,1)S(1)} %get-tuple-element.264), kind=kOutput, calls=%fused_computation.12 | convolution fusion | flops 154284032 | bytes 15622208 | tf_op jit(solution)/shard_map/ktf,fkc->ktc/dot_general | solution.py:179
  191.2 0.9 reshape.223
  192.2 125.3 %all-reduce.6.cloned.1.call-done = f32[320,512]{1,0:T(8,128)} async-done(((f32[320,512]{1,0:T(8,128)}), f32[320,512]{1,0:T(8,128)}) %all-reduce.6.cloned.1.call-update) | async-done | bytes 655376
  317.5 0.8 constant_dynamic-slice_fusion.2
  (111 shorter events, 14.0 us)
Async XLA Ops:
  7.2 16.4 %copy-start.2 = (bf16[2,5,512]{2,0,1:T(2,128)(2,1)S(1)}, bf16[2,5,512]{2,0,1:T(2,128)(2,1)}, u32[]{:S(2)}) copy-start(bf16[2,5,512]{2,0,1:T(2,128)(2,1)} %param.14) | copy-start | bytes 30724
  7.2 4.7 %copy-start.6 = (s32[4]{0:T(128)S(1)}, s32[4]{0:T(128)}, u32[]{:S(2)}) copy-start(s32[4]{0:T(128)} %param.25) | copy-start | bytes 52
  7.2 6.6 %copy-start.5 = (s32[4]{0:T(128)S(1)}, s32[4]{0:T(128)}, u32[]{:S(2)}) copy-start(s32[4]{0:T(128)} %param.24) | copy-start | bytes 52
  7.2 10.5 %copy-start = (bf16[2,128,2048]{2,1,0:T(8,128)(2,1)S(1)}, bf16[2,128,2048]{2,1,0:T(8,128)(2,1)}, u32[]{:S(2)}) copy-start(bf16[2,128,2048]{2,1,0:T(8,128)(2,1)} %param.22) | copy-start | bytes 3145732
  7.2 35.4 %copy-start.7 = (s32[2]{0:T(128)S(1)}, s32[2]{0:T(128)}, u32[]{:S(2)}) copy-start(s32[2]{0:T(128)} %param.23) | copy-start | bytes 28
  7.2 63.1 %all-reduce.4.cloned.1.call-start = ((), (), s32[]{:S(2)}) async-start(), calls=%async_computation.1 | async-start | bytes 786432 | tf_op jit(solution)/shard_map/psum | solution.py:101
  18.4 53.5 %all-to-all-start = ((bf16[4,16,2048]{2,1,0:T(8,128)(2,1)}), bf16[4,16,2048]{2,1,0:T(8,128)(2,1)S(1)}, u32[]{:S(2)}, u32[]{:S(2)}) async-start(bf16[4,16,2048]{2,1,0:T(8,128)(2,1)} %dynamic-slice_dynamic-update-slice_fusion), calls=%async_computation | async-start | bytes 524288 | tf_op jit(solution)/shard_map/all_to_all | solution.py:92
  23.5 96.7 %all-gather.6.cloned.1.call-start = ((), (), s32[]{:S(2)}) async-start(), calls=%async_computation.2 | async-start | bytes 1474560 | tf_op jit(solution)/shard_map/all_gather | solution.py:19
  71.9 8.2 %copy-start.1 = (bf16[1,16,2048]{2,1,0:T(8,128)(2,1)}, bf16[1,16,2048]{2,1,0:T(8,128)(2,1)S(1)}, u32[]{:S(2)}) copy-start(bf16[1,16,2048]{2,1,0:T(8,128)(2,1)S(1)} %constant_dynamic-slice_fusion.1) | copy-start | bytes 196612
  75.0 5.0 %copy-start.3 = (f32[4096]{0:T(1024)S(1)}, f32[4096]{0:T(1024)}, u32[]{:S(2)}) copy-start(f32[4096]{0:T(1024)} %param.18) | copy-start | bytes 49156
  75.9 241.6 %all-reduce.6.cloned.1.call-start = ((), (), s32[]{:S(2)}) async-start(), calls=%async_computation.3 | async-start | bytes 1310720
  179.6 3.4 %copy-start.4 = (bf16[4096,448]{0,1:T(8,128)(2,1)S(1)}, bf16[4096,448]{0,1:T(8,128)(2,1)}, u32[]{:S(2)}) copy-start(bf16[4096,448]{0,1:T(8,128)(2,1)} %param.20) | copy-start | bytes 11010052
Sparse Core Ops, SparseCore 0:
  12.0 58.2 all-reduce.3
  76.0 23.0 all-gather.5
  192.3 125.1 all-reduce.5
where the time goes:
time: 326 us; the launch traced here: 325 us
  waiting for transfers between devices  152 us (47%)
  blocking collectives  86.3 us (26%)
  local copies, waits for them, and re-layouts  34.3 us (11%)
  matrix products  20.4 us (6%)
  between operations  19.9 us (6%)
  other arithmetic  7.03 us (2%)
  starting transfers between devices  5.26 us (2%)
    unnamed x4, waiting for transfers between devices  125 us
    all_gather x1, blocking collectives, body(): lax.all_gather(residual[None], ('req', 'mlp'), axis=0, tiled=True)  41.9 us
    all_gather x2, blocking collectives, merged_2(): everything = jax.tree.map(lambda part: lax.all_gather(part, axis), shard)  28 us
    psum x1, waiting for transfers between devices, body(): square_sum, projected = lax.psum((square_part, projected), 'mlp')  26.7 us
    psum x1, blocking collectives, body(): square_sum, projected = lax.psum((square_part, projected), 'mlp')  16.4 us
    gather x1, local copies, waits for them, and re-layouts, body(): col_sel = jnp.take(down_cols, block_index % block_count, axis=1)  9.3 us
    dynamic_slice x7, local copies, waits for them, and re-layouts, lap(): return combine(so_far, jax.tree.map(lambda part: part[k], everything))  6.53 us
  transfers between devices with their start and end apart: 4, of which 2 were waited for; matrix products, arithmetic and copies ran while one was open for 7% of the time, Pallas kernels for 0%

commit v1 on v0

v1 whole, which is shorter than its diff:
```python
import functools

import jax
import jax.numpy as jnp
import numpy as np
from jax import lax
from jax.experimental import pallas as pl
from jax.experimental.pallas import tpu as pltpu
from jax.sharding import PartitionSpec as P

HEADS = 32
KVH = 8
HD = 128
MIG_ROWS = 16
EPSILON = 1e-05
ROPE_BASE = 500000.0
NEG_FILL = -1e30
SLOT_ROWS = 8
ROWS = 16
F32 = jnp.float32
BF16 = jnp.bfloat16


def aligned(index, multiple):
    return pl.multiple_of(index, multiple)


def loop(start, stop, step):
    def lap(k, carry):
        step(k)
        return carry

    lax.fori_loop(start, stop, lap, 0)


def dot(a, b):
    return jnp.dot(a, b, preferred_element_type=F32)


def dot_t(a, b):
    return lax.dot_general(a, b, (((1,), (1,)), ((), ())), preferred_element_type=F32)


def softmax_part(queries, keys, values, usable):
    scores = dot_t(queries, keys) * (HD ** (-0.5))
    highest = jnp.max(jnp.where(usable, scores, NEG_FILL), axis=-1, keepdims=True)
    weights = jnp.where(usable, jnp.exp(scores - highest), 0.0)
    return highest, jnp.sum(weights, axis=-1, keepdims=True), dot(weights.astype(BF16), values)


def stat_rows(highest, summed):
    rows = highest.shape[0]
    lane = lax.broadcasted_iota(jnp.int32, (rows, 128), 1)
    wide = jnp.where(lane % 2 == 0, highest, summed)
    if rows < 128:
        wide = jnp.concatenate([wide, jnp.zeros((128 - rows, 128), F32)], axis=0)
    return jnp.transpose(wide)[:8]


def kernel(
    G,
    B,
    spec_len,
    lengths,
    mig_slot,
    mig_dest,
    freq,
    hidden_h,
    again_h,
    wqkv_h,
    wout_h,
    mgain_h,
    wgate_h,
    wup_h,
    wdown_h,
    kv_h,
    out,
    moved_h,
    hid,
    again,
    wqkv,
    wout,
    mgain,
    wgate,
    wup,
    wdown,
    kv,
    xs,
    kvp,
    p_send,
    p_recv,
    mig_send,
    mig_recv,
    moved,
    q_all,
    acc_send,
    acc_recv,
    st_send,
    st_recv,
    rates,
    att_all,
    res_all,
    act,
    d_send,
    d_recv,
    e_send,
    e_recv,
    ld_sem,
    p_ss,
    p_rs,
    m_ss,
    m_rs,
    q_ss,
    q_rs,
    a_ss,
    a_rs,
    t_ss,
    t_rs,
    o_ss,
    o_rs,
    r_ss,
    r_rs,
    f_ss,
    f_rs,
    d_ss,
    d_rs,
    e_ss,
    e_rs,
):
    me_r = lax.axis_index("req")
    me_b = lax.axis_index("mlp")
    W = hid.shape[2]
    D = W * B
    QW = HEADS * HD // B
    HQ = HEADS // B
    REP = B // KVH
    SR = HQ * SLOT_ROWS
    RQ = 2 * SR
    KV0 = HEADS * HD

    def peer_b(j):
        return lax.rem(me_b + j, B)

    def from_b(j):
        return lax.rem(me_b + B - j, B)

    def peer_r(j):
        return lax.rem(me_r + j, G)

    def from_r(j):
        return lax.rem(me_r + G - j, G)

    def to_mlp(src, dst, ss, rs, j):
        return pltpu.make_async_remote_copy(
            src_ref=src, dst_ref=dst, send_sem=ss, recv_sem=rs,
            device_id={"mlp": peer_b(j)}, device_id_type=pl.DeviceIdType.MESH,
        )

    def to_req(src, dst, ss, rs, j):
        return pltpu.make_async_remote_copy(
            src_ref=src, dst_ref=dst, send_sem=ss, recv_sem=rs,
            device_id={"req": peer_r(j)}, device_id_type=pl.DeviceIdType.MESH,
        )

    loads = [
        pltpu.make_async_copy(src, dst, ld_sem.at[i])
        for i, (src, dst) in enumerate(
            [
                (hidden_h, hid),
                (again_h, again),
                (wqkv_h, wqkv),
                (kv_h, kv),
                (wout_h, wout),
                (mgain_h, mgain),
                (wgate_h, wgate),
                (wup_h, wup),
                (wdown_h, wdown),
            ]
        )
    ]
    for load in loads[:4]:
        load.start()

    barrier = pltpu.get_barrier_semaphore()
    for j in range(1, B):
        pl.semaphore_signal(
            barrier, inc=1, device_id={"mlp": peer_b(j)}, device_id_type=pl.DeviceIdType.MESH
        )
    for j in range(1, G):
        pl.semaphore_signal(
            barrier, inc=1, device_id={"req": peer_r(j)}, device_id_type=pl.DeviceIdType.MESH
        )

    xs[...] = jnp.zeros_like(xs)
    loads[0].wait()
    loads[1].wait()
    for t in range(spec_len):
        both = hid[t].astype(F32)
        for s in range(2):
            xs[s * SLOT_ROWS + t : s * SLOT_ROWS + t + 1, :] = both[s : s + 1]
    x = xs[...]
    square = jnp.sum(x * x, axis=-1, keepdims=True)
    scaled = (x * again[...]).astype(BF16)
    lane = lax.broadcasted_iota(jnp.int32, (ROWS, 128), 1)
    high = jnp.broadcast_to(square, (ROWS, 128)).astype(BF16).astype(F32)
    square_cols = jnp.where(lane < 64, high, square - high).astype(BF16)
    loads[2].wait()
    for load in loads[4:]:
        load.start()
    kvp[...] = dot(scaled, wqkv[:, KV0:]).astype(BF16)

    def project(d, slot):
        head = lax.div(d, REP)
        p_send[slot, :, :QW] = dot(scaled, wqkv[:, pl.ds(aligned(d * QW, 128), QW)]).astype(BF16)
        p_send[slot, :, QW : QW + HD] = kvp[:, pl.ds(aligned(head * HD, 128), HD)]
        p_send[slot, :, QW + HD : QW + 2 * HD] = kvp[:, pl.ds(aligned((KVH + head) * HD, 128), HD)]
        p_send[slot, :, QW + 2 * HD :] = square_cols

    def p_copy(j):
        return to_mlp(p_send.at[j], p_recv.at[j], p_ss.at[j], p_rs.at[j], j)

    pl.semaphore_wait(barrier, B + G - 2)

    def p_step(j):
        project(peer_b(j), j)
        p_copy(j).start()

    loop(1, B, p_step)
    project(me_b, 0)

    loads[3].wait()
    own_slot = mig_slot[me_r]
    kv_w = kv.shape[2]
    slot_of = jnp.full((MIG_ROWS, kv_w), own_slot, jnp.int32)
    leaving = jnp.where(
        slot_of == 0, kv[0, :MIG_ROWS, :].astype(F32), kv[1, :MIG_ROWS, :].astype(F32)
    )
    mig_send[...] = leaving.astype(BF16)

    def m_copy(j):
        return to_req(mig_send, mig_recv.at[j], m_ss.at[j], m_rs.at[j], j)

    for j in range(1, G):
        m_copy(j).start()

    row = lax.broadcasted_iota(jnp.int32, (ROWS, 128), 0)
    first = row < SLOT_ROWS
    position = jnp.where(
        first, jnp.full((ROWS, 128), lengths[0], jnp.int32) + row,
        jnp.full((ROWS, 128), lengths[1], jnp.int32) + (row - SLOT_ROWS),
    )
    angle = position.astype(F32) * freq[...]
    cos_part = jnp.cos(angle)
    sin_part = jnp.where(lane < HD // 2, -jnp.sin(angle), jnp.sin(angle))

    def rotate(v):
        return v * cos_part + pltpu.roll(v, HD // 2, 1) * sin_part

    total = p_send[0].astype(F32)
    for j in range(1, B):
        p_copy(j).wait_recv()
        total = total + p_recv[j].astype(F32)
    last = total[:, QW + 2 * HD :]
    square_sum = jnp.sum(
        jnp.where((lane == 0) | (lane == 64), last, 0.0), axis=-1, keepdims=True
    )
    projected = total[:, : QW + 2 * HD] * lax.rsqrt(square_sum / D + EPSILON)
    heads = [rotate(projected[:, n * HD : (n + 1) * HD]) for n in range(HQ)]
    own_q = jnp.concatenate(
        [
            heads[n][s * SLOT_ROWS : (s + 1) * SLOT_ROWS]
            for s in range(2)
            for n in range(HQ)
        ],
        axis=0,
    ).astype(BF16)
    q_all[me_b] = own_q

    def q_copy(j):
        return to_mlp(q_all.at[me_b], q_all.at[me_b], q_ss.at[j], q_rs.at[j], j)

    def q_arrival(j):
        b = from_b(j)
        return to_mlp(q_all.at[b], q_all.at[b], q_ss.at[j], q_rs.at[j], j)

    for j in range(1, B):
        q_copy(j).start()

    pad = jnp.zeros((128 - ROWS, HD), F32)
    new_k = jnp.concatenate([rotate(projected[:, QW : QW + HD]), pad], axis=0).astype(BF16)
    new_v = jnp.concatenate([projected[:, QW + HD :], pad], axis=0).astype(BF16)
    r_i = lax.broadcasted_iota(jnp.int32, (RQ, 128), 0)
    c_i = lax.broadcasted_iota(jnp.int32, (RQ, 128), 1)
    same = (r_i // SR) == (c_i // SLOT_ROWS)
    causal = same & ((c_i % SLOT_ROWS) <= (r_i % SLOT_ROWS))
    own_max, own_sum, own_acc = softmax_part(own_q, new_k, new_v, causal)
    own_stats = stat_rows(own_max, own_sum)

    arrived = jnp.where(
        jnp.full((MIG_ROWS, kv_w), mig_dest[me_r], jnp.int32) == me_r,
        mig_send[...].astype(F32), 0.0,
    )
    for j in range(1, G):
        m_copy(j).wait_recv()
        arrived = jnp.where(
            jnp.full((MIG_ROWS, kv_w), mig_dest[from_r(j)], jnp.int32) == me_r,
            mig_recv[j].astype(F32), arrived,
        )
    moved[0] = arrived.astype(BF16)
    moved_copy = pltpu.make_async_copy(moved, moved_h, ld_sem.at[len(loads)])
    moved_copy.start()
    for s in range(2):
        kv[s, :MIG_ROWS, :] = jnp.where(
            slot_of == s, arrived, kv[s, :MIG_ROWS, :].astype(F32)
        ).astype(BF16)

    stored = lax.broadcasted_iota(jnp.int32, (SR, kv.shape[1]), 1) * B + me_b
    usable = [stored < jnp.full(stored.shape, lengths[s], jnp.int32) for s in range(2)]

    def attend(b, slot):
        head = lax.div(b, REP)
        k_at = pl.ds(aligned(head * HD, 128), HD)
        v_at = pl.ds(aligned((KVH + head) * HD, 128), HD)
        q = q_all[b]
        parts = [
            softmax_part(q[s * SR : (s + 1) * SR], kv[s, :, k_at], kv[s, :, v_at], usable[s])
            for s in range(2)
        ]
        high_c, sum_c, acc = [
            jnp.concatenate([parts[0][i], parts[1][i]], axis=0) for i in range(3)
        ]
        acc_send[slot] = acc.astype(BF16)
        st_send[slot] = stat_rows(high_c, sum_c)

    def a_copy(j):
        return pltpu.make_async_remote_copy(
            src_ref=acc_send.at[j], dst_ref=acc_recv.at[j], send_sem=a_ss.at[j],
            recv_sem=a_rs.at[j], device_id={"mlp": from_b(j)},
            device_id_type=pl.DeviceIdType.MESH,
        )

    def t_copy(j):
        return pltpu.make_async_remote_copy(
            src_ref=st_send.at[j], dst_ref=st_recv.at[j], send_sem=t_ss.at[j],
            recv_sem=t_rs.at[j], device_id={"mlp": from_b(j)},
            device_id_type=pl.DeviceIdType.MESH,
        )

    def a_step(j):
        q_arrival(j).wait_recv()
        attend(from_b(j), j)
        a_copy(j).start()
        t_copy(j).start()

    loop(1, B, a_step)
    attend(me_b, 0)

    stats = [own_stats, st_send[0]]
    for j in range(1, B):
        t_copy(j).wait_recv()
        stats.append(st_recv[j])
    top = functools.reduce(jnp.maximum, [s[0:1] for s in stats])
    scales = [jnp.exp(s[0:1] - top) for s in stats]
    summed = functools.reduce(jnp.add, [e * s[1:2] for e, s in zip(scales, stats)])
    rates[...] = jnp.zeros_like(rates)
    for i, e in enumerate(scales):
        rates[i : i + 1, :] = e / summed
    columns = jnp.transpose(rates[...])
    mixture = own_acc * columns[:RQ, 0:1] + acc_send[0].astype(F32) * columns[:RQ, 1:2]
    for j in range(1, B):
        a_copy(j).wait_recv()
        mixture = mixture + acc_recv[j].astype(F32) * columns[:RQ, j + 1 : j + 2]
    attended = jnp.concatenate(
        [
            jnp.concatenate(
                [
                    mixture[s * SR + n * SLOT_ROWS : s * SR + (n + 1) * SLOT_ROWS]
                    for s in range(2)
                ],
                axis=0,
            )
            for n in range(HQ)
        ],
        axis=1,
    ).astype(BF16)
    att_all[0] = attended

    def o_copy(j):
        return to_mlp(att_all.at[0], att_all.at[j], o_ss.at[j], o_rs.at[j], j)

    for j in range(1, B):
        o_copy(j).start()

    loads[4].wait()

    def out_part(b, slot):
        return dot(att_all[slot], wout[pl.ds(aligned(b * QW, 128), QW), :])

    def o_step(j, so_far):
        o_copy(j).wait_recv()
        return so_far + out_part(from_b(j), j)

    attn_out = lax.fori_loop(1, B, o_step, out_part(me_b, 0))
    residual = (xs[...] + attn_out).astype(BF16)

    res_all[me_r, me_b] = residual

    def r_copy(j):
        here = res_all.at[me_r, me_b]
        return to_mlp(here, here, r_ss.at[j], r_rs.at[j], j)

    def r_arrival(j):
        here = res_all.at[me_r, from_b(j)]
        return to_mlp(here, here, r_ss.at[j], r_rs.at[j], j)

    def f_copy(i, j, b):
        here = res_all.at[me_r, b]
        return to_req(here, here, f_ss.at[i, j], f_rs.at[i, j], i)

    def f_arrival(i, j):
        here = res_all.at[from_r(i), from_b(j)]
        return to_req(here, here, f_ss.at[i, j], f_rs.at[i, j], i)

    for j in range(1, B):
        r_copy(j).start()
    for i in range(1, G):
        f_copy(i, 0, me_b).start()

    def f_step(j):
        r_arrival(j).wait_recv()
        for i in range(1, G):
            f_copy(i, j, from_b(j)).start()

    loop(1, B, f_step)

    loads[5].wait()
    loads[6].wait()
    loads[7].wait()
    M = G * ROWS
    F = wgate.shape[0]

    def up_step(j, carry):
        sq, gate, up = carry
        b = from_b(j)
        block = res_all[:, b].reshape(M, W).astype(F32)
        sq = sq + jnp.sum(block * block, axis=-1, keepdims=True)
        rows = (block * mgain[:, pl.ds(aligned(b * W, 128), W)]).astype(BF16)
        depth = pl.ds(aligned(b * W, 128), W)
        return sq, gate + dot_t(rows, wgate[:, depth]), up + dot_t(rows, wup[:, depth])

    def up_lap(j, carry):
        for i in range(1, G):
            f_arrival(i, j).wait_recv()
        return up_step(j, carry)

    zero = jnp.zeros((M, F), F32)
    sq, gate, up = lax.fori_loop(0, B, up_lap, (jnp.zeros((M, 1), F32), zero, zero))
    inverse = lax.rsqrt(sq / D + EPSILON)
    gate = gate * inverse
    up = up * inverse
    act[...] = (gate / (1.0 + jnp.exp(-gate)) * up).astype(BF16)

    loads[8].wait()

    def d_copy(i, j):
        return to_req(
            d_send.at[j, peer_r(i)], d_recv.at[j, i], d_ss.at[i, j], d_rs.at[i, j], i
        )

    def d_step(k):
        j = lax.rem(k + 1, B)
        b = peer_b(j)
        part = dot(act[...], wdown[:, pl.ds(aligned(b * W, 128), W)])
        d_send[j] = part.astype(BF16).reshape(G, ROWS, W)
        for i in range(1, G):
            d_copy(i, j).start()

    loop(0, B, d_step)

    def e_copy(j):
        return to_mlp(e_send.at[j], e_recv.at[j], e_ss.at[j], e_rs.at[j], j)

    def summed_block(j):
        so_far = d_send[j, me_r].astype(F32)
        for i in range(1, G):
            d_copy(i, j).wait_recv()
            so_far = so_far + d_recv[j, i].astype(F32)
        return so_far

    def e_step(j):
        e_send[j] = summed_block(j).astype(BF16)
        e_copy(j).start()

    loop(1, B, e_step)
    result = res_all[me_r, me_b].astype(F32) + summed_block(0)
    for j in range(1, B):
        e_copy(j).wait_recv()
        result = result + e_recv[j].astype(F32)
    for t in range(spec_len):
        out[t] = jnp.concatenate(
            [result[s * SLOT_ROWS + t : s * SLOT_ROWS + t + 1] for s in range(2)], axis=0
        ).astype(BF16)

    moved_copy.wait()
    for j in range(1, G):
        m_copy(j).wait_send()

    def drain(j):
        p_copy(j).wait_send()
        q_copy(j).wait_send()
        a_copy(j).wait_send()
        t_copy(j).wait_send()
        o_copy(j).wait_send()
        r_copy(j).wait_send()
        e_copy(j).wait_send()

    loop(1, B, drain)

    def drain_req(j):
        for i in range(1, G):
            f_copy(i, j, from_b(j)).wait_send()
            d_copy(i, j).wait_send()

    loop(0, B, drain_req)


def body(
    hidden, attn_gain, w_qkv, w_out, mlp_gain, w_gate, w_up, w_down,
    kv_cache, lengths, mig_slot, mig_dest,
):
    G = lax.axis_size("req")
    B = lax.axis_size("mlp")
    slots, spec_len, W = hidden.shape
    QW = HEADS * HD // B
    RQ = 2 * (HEADS // B) * SLOT_ROWS
    CW = QW + 3 * HD
    kv_w = kv_cache.shape[2]
    F = w_gate.shape[1]
    w_gate, w_up = w_gate.T, w_up.T
    hidden = hidden.transpose(1, 0, 2)
    half = HD // 2
    freq = np.float32(ROPE_BASE) ** (-(np.arange(half, dtype=np.float32) / np.float32(half)))
    freq = jnp.asarray(np.concatenate([freq, freq])[None, :], F32)
    anywhere = pl.BlockSpec(memory_space=pl.ANY)
    smem = pl.BlockSpec(memory_space=pltpu.SMEM)
    vmem = pl.BlockSpec(memory_space=pltpu.VMEM)
    V = pltpu.VMEM
    dma = pltpu.SemaphoreType.DMA
    scratch = [
        V(hidden.shape, BF16),
        V((1, W), F32),
        V(w_qkv.shape, BF16),
        V(w_out.shape, BF16),
        V((1, mlp_gain.shape[0]), F32),
        V(w_gate.shape, BF16),
        V(w_up.shape, BF16),
        V(w_down.shape, BF16),
        V(kv_cache.shape, BF16),
        V((ROWS, W), F32),
        V((ROWS, kv_w), BF16),
        V((B, ROWS, CW), BF16),
        V((B, ROWS, CW), BF16),
        V((MIG_ROWS, kv_w), BF16),
        V((G, MIG_ROWS, kv_w), BF16),
        V((1, MIG_ROWS, kv_w), BF16),
        V((B, RQ, HD), BF16),
        V((B, RQ, HD), BF16),
        V((B, RQ, HD), BF16),
        V((B, 8, 128), F32),
        V((B, 8, 128), F32),
        V((128, 128), F32),
        V((B, ROWS, QW), BF16),
        V((G, B, ROWS, W), BF16),
        V((G * ROWS, F), BF16),
        V((B, G, ROWS, W), BF16),
        V((B, G, ROWS, W), BF16),
        V((B, ROWS, W), BF16),
        V((B, ROWS, W), BF16),
        dma((10,)),
        dma((B,)), dma((B,)),
        dma((G,)), dma((G,)),
        dma((B,)), dma((B,)),
        dma((B,)), dma((B,)),
        dma((B,)), dma((B,)),
        dma((B,)), dma((B,)),
        dma((B,)), dma((B,)),
        dma((G, B)), dma((G, B)),
        dma((G, B)), dma((G, B)),
        dma((B,)), dma((B,)),
    ]
    layer_out, moved = pl.pallas_call(
        functools.partial(kernel, G, B, spec_len),
        out_shape=(
            jax.ShapeDtypeStruct(hidden.shape, BF16),
            jax.ShapeDtypeStruct((1, MIG_ROWS, kv_w), BF16),
        ),
        in_specs=[smem, smem, smem, vmem] + [anywhere] * 9,
        out_specs=(vmem, anywhere),
        scratch_shapes=scratch,
        compiler_params=pltpu.CompilerParams(
            collective_id=0, has_side_effects=True, vmem_limit_bytes=56 * 1024 * 1024
        ),
    )(
        lengths, mig_slot, mig_dest, freq, hidden, attn_gain.reshape(1, W), w_qkv, w_out,
        mlp_gain.reshape(1, -1), w_gate, w_up, w_down, kv_cache,
    )
    return layer_out.transpose(1, 0, 2), moved


def solution(mesh):
    placed = (
        P("req", None, "mlp"),
        P("mlp"),
        P("mlp", None),
        P(None, "mlp"),
        P(),
        P(None, ("req", "mlp")),
        P(None, ("req", "mlp")),
        P(("req", "mlp"), None),
        P("req", "mlp", None),
        P("req"),
        P(),
        P(),
    )
    return jax.shard_map(
        body,
        mesh=mesh,
        in_specs=placed,
        out_specs=(P("req", None, "mlp"), P("req", "mlp", None)),
        check_vma=False,
    )
```

time: 326 us -> 55.8 us (0.17)
  waiting for transfers between devices: 152 us -> 0 us
  blocking collectives: 86.3 us -> 0 us
  Pallas kernels: 0 us -> 52.1 us
  local copies, waits for them, and re-layouts: 34.3 us -> 2.78 us
  matrix products: 20.4 us -> 0 us
  between operations: 19.9 us -> 0.64 us
  other arithmetic: 7.03 us -> 0 us
  starting transfers between devices: 5.26 us -> 0 us
    unnamed x4 -> x0, waiting for transfers between devices: 125 us -> none
    all_gather x3 -> x0, blocking collectives: 69.9 us -> none  [the longest x1 41.9 us: body(): lax.all_gather(residual[None], ('req', 'mlp'), axis=0, tiled=True)]
    pallas_call x0 -> x1, Pallas kernels: none -> 52.1 us  [body(): pl.pallas_call(functools.partial(kernel, G, B, spec_len), out_shape=(jax....]
    psum x1 -> x0, waiting for transfers between devices: 26.7 us -> none  [body(): square_sum, projected = lax.psum((square_part, projected), 'mlp')]
    dot_general x9 -> x0, matrix products: 20.4 us -> none  [the longest x1 6.45 us: body(): jnp.einsum('ktf,fkc->ktc', row_sel, col_sel, preferred_element_type=jnp.f...]
    psum x1 -> x0, blocking collectives: 16.4 us -> none  [body(): square_sum, projected = lax.psum((square_part, projected), 'mlp')]
    gather x2 -> x0, local copies, waits for them, and re-layouts: 9.88 us -> none  [the longest x1 9.3 us: body(): col_sel = jnp.take(down_cols, block_index % block_count, axis=1)]
    dynamic_slice x10 -> x0, local copies, waits for them, and re-layouts: 7.72 us -> none  [the longest x7 6.53 us: lap(): return combine(so_far, jax.tree.map(lambda part: part[k], everything))]
  transfers between devices with their start and end apart: 4 -> 0, of which waited for: 2 -> 0; matrix products, arithmetic and copies ran while one was open for 7% -> 0% of each run, Pallas kernels for 0% -> 0%
where the time goes in v1:
time: 55.8 us; the launch traced here: 55.5 us
  Pallas kernels  52.1 us (93%)
  local copies, waits for them, and re-layouts  2.78 us (5%)
  between operations  0.64 us (1%)
    pallas_call x1, Pallas kernels, body(): pl.pallas_call(functools.partial(kernel, G, B, spec_len), out_shape=(jax....  52.1 us
    unnamed x2, local copies, waits for them, and re-layouts  2.78 us

profile of v1, /device:TPU:0, one launch (start us, length us, event | category | flops | bytes accessed | tf_op | source)
XLA Modules:
  0.0 55.5 jit_solution(12192610071386791268)
XLA Ops:
  0.6 52.1 %shard_map.140 = (bf16[5,2,512]{2,1,0:T(2,128)(2,1)}, bf16[1,16,2048]{2,1,0:T(8,128)(2,1)}) custom-call(s32[2]{0:T(128)} %lengths.1, s32[4]{0:T(128)} %mig_slot.1, s32[4]{0:T(128)} %mig_dest.1, f32[1,128]{1,0:T(1,128)} %constant.2.clone.freq, bf16[5,2,512]{2,1,0:T(2,128)(2,1)} %bitcast.9, f32[1,512]{1,0:T(1,128)} %bitcast.11, bf16[512,6144]{1,0:T(8,128)(2,1)} %wqkv_h.1, ...), custom_call_target="tpu_custom_call" | custom-call | tf_op jit(solution)/shard_map/pallas_call | solution.py:591
  52.7 1.3 %copy.17 = bf16[2,5,512]{2,0,1:T(2,128)(2,1)} copy(bf16[2,5,512]{2,0,1:T(2,128)(2,1)} %bitcast.10) | data formatting | bytes 20480
  54.0 1.5 %copy.18 = bf16[1,16,2048]{2,1,0:T(8,128)(2,1)} copy(bf16[1,16,2048]{2,1,0:T(8,128)(2,1)} %get-tuple-element.9) | data formatting | bytes 131072

commit v2 on v1

--- a/solution.py
+++ b/solution.py
@@ -101,6 +101,9 @@
     att_all,
     res_all,
     act,
+    c_send,
+    c_recv,
+    d_own,
     d_send,
     d_recv,
     e_send,
@@ -122,6 +125,10 @@
     r_rs,
     f_ss,
     f_rs,
+    s_ss,
+    s_rs,
+    c_ss,
+    c_rs,
     d_ss,
     d_rs,
     e_ss,
@@ -403,35 +410,65 @@
     attn_out = lax.fori_loop(1, B, o_step, out_part(me_b, 0))
     residual = (xs[...] + attn_out).astype(BF16)
 
+    Z = B // 2
+    core = lax.rem(me_b, 2)
+    my_z = lax.div(me_b, 2)
+    sibling = my_z * 2 + (1 - core)
+
+    def peer_z(j):
+        return lax.rem(my_z + j, Z) * 2 + core
+
+    def from_z(j):
+        return lax.rem(my_z + Z - j, Z) * 2 + core
+
+    def other_core(b):
+        return b + 1 - 2 * core
+
+    def to_b(src, dst, ss, rs, b):
+        return pltpu.make_async_remote_copy(
+            src_ref=src, dst_ref=dst, send_sem=ss, recv_sem=rs,
+            device_id={"mlp": b}, device_id_type=pl.DeviceIdType.MESH,
+        )
+
     res_all[me_r, me_b] = residual
 
     def r_copy(j):
         here = res_all.at[me_r, me_b]
-        return to_mlp(here, here, r_ss.at[j], r_rs.at[j], j)
+        return to_b(here, here, r_ss.at[j], r_rs.at[j], peer_z(j))
 
     def r_arrival(j):
-        here = res_all.at[me_r, from_b(j)]
-        return to_mlp(here, here, r_ss.at[j], r_rs.at[j], j)
-
-    def f_copy(i, j, b):
-        here = res_all.at[me_r, b]
+        here = res_all.at[me_r, from_z(j)]
+        return to_b(here, here, r_ss.at[j], r_rs.at[j], peer_z(j))
+
+    def f_copy(i, j):
+        here = res_all.at[me_r, from_z(j)]
         return to_req(here, here, f_ss.at[i, j], f_rs.at[i, j], i)
 
     def f_arrival(i, j):
-        here = res_all.at[from_r(i), from_b(j)]
+        here = res_all.at[from_r(i), from_z(j)]
         return to_req(here, here, f_ss.at[i, j], f_rs.at[i, j], i)
 
-    for j in range(1, B):
+    def s_copy(i, j):
+        here = res_all.at[from_r(i), from_z(j)]
+        return to_b(here, here, s_ss.at[i, j], s_rs.at[i, j], sibling)
+
+    def s_arrival(i, j):
+        here = res_all.at[from_r(i), other_core(from_z(j))]
+        return to_b(here, here, s_ss.at[i, j], s_rs.at[i, j], sibling)
+
+    for j in range(1, Z):
         r_copy(j).start()
     for i in range(1, G):
-        f_copy(i, 0, me_b).start()
+        f_copy(i, 0).start()
+    s_copy(0, 0).start()
 
     def f_step(j):
         r_arrival(j).wait_recv()
         for i in range(1, G):
-            f_copy(i, j, from_b(j)).start()
-
-    loop(1, B, f_step)
+            f_copy(i, j).start()
+        s_copy(0, j).start()
+
+    loop(1, Z, f_step)
 
     loads[5].wait()
     loads[6].wait()
@@ -439,22 +476,28 @@
     M = G * ROWS
     F = wgate.shape[0]
 
-    def up_step(j, carry):
+    def up_step(b, carry):
         sq, gate, up = carry
-        b = from_b(j)
         block = res_all[:, b].reshape(M, W).astype(F32)
         sq = sq + jnp.sum(block * block, axis=-1, keepdims=True)
-        rows = (block * mgain[:, pl.ds(aligned(b * W, 128), W)]).astype(BF16)
         depth = pl.ds(aligned(b * W, 128), W)
+        rows = (block * mgain[:, depth]).astype(BF16)
         return sq, gate + dot_t(rows, wgate[:, depth]), up + dot_t(rows, wup[:, depth])
 
     def up_lap(j, carry):
         for i in range(1, G):
             f_arrival(i, j).wait_recv()
-        return up_step(j, carry)
+            s_copy(i, j).start()
+        return up_step(from_z(j), carry)
+
+    def up_lap_other(j, carry):
+        for i in range(G):
+            s_arrival(i, j).wait_recv()
+        return up_step(other_core(from_z(j)), carry)
 
     zero = jnp.zeros((M, F), F32)
-    sq, gate, up = lax.fori_loop(0, B, up_lap, (jnp.zeros((M, 1), F32), zero, zero))
+    sums = lax.fori_loop(0, Z, up_lap, (jnp.zeros((M, 1), F32), zero, zero))
+    sq, gate, up = lax.fori_loop(0, Z, up_lap_other, sums)
     inverse = lax.rsqrt(sq / D + EPSILON)
     gate = gate * inverse
     up = up * inverse
@@ -462,26 +505,41 @@
 
     loads[8].wait()
 
+    def down_part(b):
+        return dot(act[...], wdown[:, pl.ds(aligned(b * W, 128), W)])
+
+    def c_copy(j):
+        return to_b(c_send.at[j], c_recv.at[j], c_ss.at[j], c_rs.at[j], sibling)
+
+    def c_step(k):
+        j = lax.rem(k + 1, Z)
+        c_send[j] = down_part(other_core(peer_z(j)))
+        c_copy(j).start()
+
+    loop(0, Z, c_step)
+
     def d_copy(i, j):
         return to_req(
             d_send.at[j, peer_r(i)], d_recv.at[j, i], d_ss.at[i, j], d_rs.at[i, j], i
         )
 
     def d_step(k):
-        j = lax.rem(k + 1, B)
-        b = peer_b(j)
-        part = dot(act[...], wdown[:, pl.ds(aligned(b * W, 128), W)])
-        d_send[j] = part.astype(BF16).reshape(G, ROWS, W)
+        j = lax.rem(k + 1, Z)
+        part = down_part(peer_z(j))
+        c_copy(j).wait_recv()
+        part = (part + c_recv[j]).reshape(G, ROWS, W)
+        d_own[j] = part
+        d_send[j] = part.astype(BF16)
         for i in range(1, G):
             d_copy(i, j).start()
 
-    loop(0, B, d_step)
+    loop(0, Z, d_step)
 
     def e_copy(j):
-        return to_mlp(e_send.at[j], e_recv.at[j], e_ss.at[j], e_rs.at[j], j)
+        return to_b(e_send.at[j], e_recv.at[j], e_ss.at[j], e_rs.at[j], peer_z(j))
 
     def summed_block(j):
-        so_far = d_send[j, me_r].astype(F32)
+        so_far = d_own[j, me_r]
         for i in range(1, G):
             d_copy(i, j).wait_recv()
             so_far = so_far + d_recv[j, i].astype(F32)
@@ -491,9 +549,9 @@
         e_send[j] = summed_block(j).astype(BF16)
         e_copy(j).start()
 
-    loop(1, B, e_step)
+    loop(1, Z, e_step)
     result = res_all[me_r, me_b].astype(F32) + summed_block(0)
-    for j in range(1, B):
+    for j in range(1, Z):
         e_copy(j).wait_recv()
         result = result + e_recv[j].astype(F32)
     for t in range(spec_len):
@@ -511,17 +569,24 @@
         a_copy(j).wait_send()
         t_copy(j).wait_send()
         o_copy(j).wait_send()
+
+    loop(1, B, drain)
+
+    def drain_z(j):
         r_copy(j).wait_send()
         e_copy(j).wait_send()
 
-    loop(1, B, drain)
+    loop(1, Z, drain_z)
 
     def drain_req(j):
+        c_copy(j).wait_send()
+        s_copy(0, j).wait_send()
         for i in range(1, G):
-            f_copy(i, j, from_b(j)).wait_send()
+            f_copy(i, j).wait_send()
+            s_copy(i, j).wait_send()
             d_copy(i, j).wait_send()
 
-    loop(0, B, drain_req)
+    loop(0, Z, drain_req)
 
 
 def body(
@@ -530,6 +595,7 @@
 ):
     G = lax.axis_size("req")
     B = lax.axis_size("mlp")
+    Z = B // 2
     slots, spec_len, W = hidden.shape
     QW = HEADS * HD // B
     RQ = 2 * (HEADS // B) * SLOT_ROWS
@@ -572,10 +638,13 @@
         V((B, ROWS, QW), BF16),
         V((G, B, ROWS, W), BF16),
         V((G * ROWS, F), BF16),
-        V((B, G, ROWS, W), BF16),
-        V((B, G, ROWS, W), BF16),
-        V((B, ROWS, W), BF16),
-        V((B, ROWS, W), BF16),
+        V((Z, G * ROWS, W), F32),
+        V((Z, G * ROWS, W), F32),
+        V((Z, G, ROWS, W), F32),
+        V((Z, G, ROWS, W), BF16),
+        V((Z, G, ROWS, W), BF16),
+        V((Z, ROWS, W), BF16),
+        V((Z, ROWS, W), BF16),
         dma((10,)),
         dma((B,)), dma((B,)),
         dma((G,)), dma((G,)),
@@ -583,10 +652,12 @@
         dma((B,)), dma((B,)),
         dma((B,)), dma((B,)),
         dma((B,)), dma((B,)),
-        dma((B,)), dma((B,)),
-        dma((G, B)), dma((G, B)),
-        dma((G, B)), dma((G, B)),
-        dma((B,)), dma((B,)),
+        dma((Z,)), dma((Z,)),
+        dma((G, Z)), dma((G, Z)),
+        dma((G, Z)), dma((G, Z)),
+        dma((Z,)), dma((Z,)),
+        dma((G, Z)), dma((G, Z)),
+        dma((Z,)), dma((Z,)),
     ]
     layer_out, moved = pl.pallas_call(
         functools.partial(kernel, G, B, spec_len),

time: 55.8 us -> 54.6 us (0.978)
  Pallas kernels: 52.1 us -> 50.9 us
    pallas_call x1, Pallas kernels: 52.1 us -> 50.9 us  [body(): pl.pallas_call(functools.partial(kernel, G, B, spec_len), out_shape=(jax....]
where the time goes in v2:
time: 54.6 us; the launch traced here: 54.3 us
  Pallas kernels  50.9 us (93%)
  local copies, waits for them, and re-layouts  2.78 us (5%)
  between operations  0.64 us (1%)
    pallas_call x1, Pallas kernels, body(): pl.pallas_call(functools.partial(kernel, G, B, spec_len), out_shape=(jax....  50.9 us
    unnamed x2, local copies, waits for them, and re-layouts  2.78 us

profile of v2, /device:TPU:0, one launch (start us, length us, event | category | flops | bytes accessed | tf_op | source)
XLA Modules:
  0.0 54.3 jit_solution(9836950734020088910)
XLA Ops:
  0.6 50.9 %shard_map.140 = (bf16[5,2,512]{2,1,0:T(2,128)(2,1)}, bf16[1,16,2048]{2,1,0:T(8,128)(2,1)}) custom-call(s32[2]{0:T(128)} %lengths.1, s32[4]{0:T(128)} %mig_slot.1, s32[4]{0:T(128)} %mig_dest.1, f32[1,128]{1,0:T(1,128)} %constant.2.clone.freq, bf16[5,2,512]{2,1,0:T(2,128)(2,1)} %bitcast.9, f32[1,512]{1,0:T(1,128)} %bitcast.11, bf16[512,6144]{1,0:T(8,128)(2,1)} %wqkv_h.1, ...), custom_call_target="tpu_custom_call" | custom-call | tf_op jit(solution)/shard_map/pallas_call | solution.py:662
  51.5 1.3 %copy.17 = bf16[2,5,512]{2,0,1:T(2,128)(2,1)} copy(bf16[2,5,512]{2,0,1:T(2,128)(2,1)} %bitcast.10) | data formatting | bytes 20480
  52.8 1.5 %copy.18 = bf16[1,16,2048]{2,1,0:T(8,128)(2,1)} copy(bf16[1,16,2048]{2,1,0:T(8,128)(2,1)} %get-tuple-element.9) | data formatting | bytes 131072
